TPU v7x, 1024 devices: a whole 8x8x8 slice. The times are simulated.
1024 devices in a mesh: ctx: 128 (over x, y, z_lo), tp: 8 (over z_hi, core).
Axes of the slice: x: 8, y: 8, z: 8 (z_hi: 4, z_lo: 2; z = z_hi * 2 + z_lo), core: 2. Of those that a mesh axis runs over, the one named last changes fastest.
Arguments:
- queries: bfloat16 [16384, 4096], P('ctx', 'tp'), may hold values from -128 to 128
- key_rows: bfloat16 [16384, 4096], P('ctx', 'tp'), may hold values from -6 to 6
- value_rows: bfloat16 [16384, 4096], P('ctx', 'tp'), may hold values from -6 to 6
- view_mask: int32 [128, 3], replicated, may hold values from 0 to 1, as said below
- norm_gain: float32 [4096], replicated, may hold values from 0.5 to 1.5
- normed_grad: bfloat16 [16384, 4096], P(('ctx', 'tp')), may hold values from -6 to 6
Outputs:
- normed: bfloat16 [16384, 4096], P(('ctx', 'tp'))
- query_grad: bfloat16 [16384, 4096], P('ctx', 'tp')
- key_grad: bfloat16 [16384, 4096], P('ctx', 'tp')
- value_grad: bfloat16 [16384, 4096], P('ctx', 'tp')
Inputs may be any that keep to these rules, and one draw needn't show every extreme that they name: `view_mask`: the blocks form views of consecutive blocks. Block 0 begins a view; otherwise a view begins only at blocks b with b % 4 equal to 2 or 3, and in every group of 4 blocks at least one of these two begins a view. A column is 1 exactly where its key block lies inside the grid of blocks and either is not later than the query block or lies in the query block's view.
All inputs are finite; a program needn't handle non-finite values.
Results may differ from a plain program's by a relative error of at most 0.012.
Values may be sent and summed in bfloat16 or wider, within the bound.
A program may use at most 32 MiB of HBM per device.

v0:
```python
import jax
import jax.numpy as jnp
from jax import lax
from jax.sharding import PartitionSpec as P

HSZ = 128
REACH = 2


NEGATIVE = -1e30
EPSILON = 1e-06


def with_halo(cells, sides, width):
    for axis, dim in sides:
        count = lax.axis_size(axis)
        ends = count - 1
        head = lax.slice_in_dim(cells, 0, width, axis=dim)
        tail = lax.slice_in_dim(cells, cells.shape[dim] - width, cells.shape[dim], axis=dim)
        cells = jnp.concatenate(
            [
                lax.ppermute(tail, axis, [(i, (i + 1) % count) for i in range(ends)]),
                cells,
                lax.ppermute(head, axis, [((i + 1) % count, i) for i in range(ends)]),
            ],
            axis=dim,
        )
    return cells


def passed_along(x, axis, by):
    peers = lax.axis_size(axis)
    pairs = [(i, i + by) for i in range(peers) if 0 <= i + by < peers]
    return lax.ppermute(x, axis, pairs)


def split_heads(values):
    return values.reshape(values.shape[0], -1, HSZ)


def per_device(queries, key_rows, value_rows, view_mask, norm_gain, normed_grad):
    length = queries.shape[0]
    span_blocks = 2 * REACH - 1
    rim_rows = (REACH - 1) * length
    score_scale = HSZ ** (-0.5)
    position = lax.axis_index("ctx")
    key_ext, value_ext = (
        with_halo(key_rows, (("ctx", 0),), rim_rows),
        with_halo(value_rows, (("ctx", 0),), rim_rows),
    )
    mask_row = lax.dynamic_slice_in_dim(view_mask, position, 1, 0)[0]
    key_live = jnp.repeat(mask_row, length) > 0
    q_heads = split_heads(queries)
    k_heads = split_heads(key_ext)
    v_heads = split_heads(value_ext)
    scores = (
        jnp.einsum("thd,shd->hts", q_heads, k_heads, preferred_element_type=jnp.float32)
        * score_scale
    )
    scores = jnp.where(key_live[None, None, :], scores, NEGATIVE)
    peak = jnp.max(scores, -1, keepdims=True)
    log_total = peak + jnp.log(jnp.sum(jnp.exp(scores - peak), -1, keepdims=True))
    probs = jnp.exp(scores - log_total)
    probs_low = probs.astype(jnp.bfloat16)
    out_heads = jnp.einsum(
        "hts,shd->thd", probs_low, v_heads, preferred_element_type=jnp.float32
    ).astype(jnp.bfloat16)
    attended = out_heads.reshape(length, -1)
    tiles = lax.all_to_all(attended, "tp", split_axis=0, concat_axis=1, tiled=True)
    values_f = tiles.astype(jnp.float32)
    inverse = lax.rsqrt(jnp.mean(values_f * values_f, -1, keepdims=True) + EPSILON)
    normed = (values_f * inverse * norm_gain).astype(jnp.bfloat16)
    upstream = normed_grad.astype(jnp.float32) * norm_gain
    inner_mean = jnp.mean(upstream * values_f, -1, keepdims=True)
    tile_grad = (inverse * upstream - values_f * inverse * inverse * inverse * inner_mean).astype(
        jnp.bfloat16
    )
    attended_grad = lax.all_to_all(tile_grad, "tp", split_axis=1, concat_axis=0, tiled=True)
    grad_heads = split_heads(attended_grad)
    delta = jnp.sum(grad_heads.astype(jnp.float32) * out_heads.astype(jnp.float32), -1)
    prob_grad = jnp.einsum("thd,shd->hts", grad_heads, v_heads, preferred_element_type=jnp.float32)
    score_grad = (probs * (prob_grad - delta.T[:, :, None])).astype(jnp.bfloat16)
    query_grad = (
        (
            jnp.einsum("hts,shd->thd", score_grad, k_heads, preferred_element_type=jnp.float32)
            * score_scale
        )
        .astype(jnp.bfloat16)
        .reshape(length, -1)
    )
    key_terms = (
        jnp.einsum("hts,thd->shd", score_grad, q_heads, preferred_element_type=jnp.float32)
        * score_scale
    ).reshape(span_blocks * length, -1)
    value_terms = jnp.einsum(
        "hts,thd->shd", probs_low, grad_heads, preferred_element_type=jnp.float32
    ).reshape(span_blocks * length, -1)
    key_total = key_terms[rim_rows : rim_rows + length]
    value_total = value_terms[rim_rows : rim_rows + length]
    for column in range(span_blocks):
        if column != REACH - 1:
            offset = column - (REACH - 1)
            received = passed_along(
                (
                    key_terms[column * length : (column + 1) * length],
                    value_terms[column * length : (column + 1) * length],
                ),
                "ctx",
                offset,
            )
            key_total = key_total + received[0]
            value_total = value_total + received[1]
    return (normed, query_grad, key_total.astype(jnp.bfloat16), value_total.astype(jnp.bfloat16))


def solution(mesh):
    placed = (P("ctx", "tp"), P("ctx", "tp"), P("ctx", "tp"), P(), P(), P(("ctx", "tp"), None))
    return jax.shard_map(
        per_device,
        mesh=mesh,
        in_specs=placed,
        out_specs=(P(("ctx", "tp"), None), P("ctx", "tp"), P("ctx", "tp"), P("ctx", "tp")),
        check_vma=False,
    )
```

profile of v0, /device:TPU:9, one launch (start us, length us, event | category | flops | bytes accessed | tf_op | source)
XLA Modules:
  0.0 100.2 jit_solution(15605639144383612354)
XLA Ops:
  0.7 1.1 %copy.56 = bf16[128,512]{0,1:T(8,128)(2,1)S(1)} copy(bf16[128,512]{1,0:T(8,128)(2,1)} %param.7) | data formatting | bytes 262144 | tf_op args[1]
  1.7 8.6 %collective-permute-start.3 = (bf16[128,512]{0,1:T(8,128)(2,1)S(1)}, bf16[128,512]{0,1:T(8,128)(2,1)S(1)}, u32[]{:S(2)}, u32[]{:S(2)}) collective-permute-start(bf16[128,512]{0,1:T(8,128)(2,1)S(1)} %copy.56), channel_id=1, source_target_pairs={{8,0},{16,8},{24,16},{32,24},{40,32},{48,40},{56,48},{64,56},{72,6... | collective-permute-start | bytes 393224 | tf_op jit(solution)/shard_map/ppermute | solution.py:24
  10.3 1.9 %collective-permute-start.2 = (bf16[128,512]{0,1:T(8,128)(2,1)S(1)}, bf16[128,512]{0,1:T(8,128)(2,1)S(1)}, u32[]{:S(2)}, u32[]{:S(2)}) collective-permute-start(bf16[128,512]{0,1:T(8,128)(2,1)S(1)} %copy.56), channel_id=1, source_target_pairs={{0,8},{8,16},{16,24},{24,32},{32,40},{40,48},{48,56},{56,64},{64,7... | collective-permute-start | bytes 393224 | tf_op jit(solution)/shard_map/ppermute | solution.py:22
  12.2 1.9 %collective-permute-start = (bf16[128,512]{1,0:T(8,128)(2,1)S(1)}, bf16[128,512]{1,0:T(8,128)(2,1)S(1)}, u32[]{:S(2)}, u32[]{:S(2)}) collective-permute-start(bf16[128,512]{1,0:T(8,128)(2,1)S(1)} %copy-done.2), channel_id=1, source_target_pairs={{0,8},{8,16},{16,24},{24,32},{32,40},{40,48},{48,56},{56,64},{64,7... | collective-permute-start | bytes 393224 | tf_op jit(solution)/shard_map/ppermute | solution.py:22
  14.2 7.6 %collective-permute-start.1 = (bf16[128,512]{1,0:T(8,128)(2,1)S(1)}, bf16[128,512]{1,0:T(8,128)(2,1)S(1)}, u32[]{:S(2)}, u32[]{:S(2)}) collective-permute-start(bf16[128,512]{1,0:T(8,128)(2,1)S(1)} %copy-done.2), channel_id=1, source_target_pairs={{8,0},{16,8},{24,16},{32,24},{40,32},{48,40},{56,48},{64,56},{72,6... | collective-permute-start | bytes 393224 | tf_op jit(solution)/shard_map/ppermute | solution.py:24
  21.8 0.7 copy-done.4
  22.5 0.2 fusion.13
  22.8 1.0 collective-permute-done
  23.8 2.9 %collective-permute-done.1 = bf16[128,512]{1,0:T(8,128)(2,1)S(1)} collective-permute-done((bf16[128,512]{1,0:T(8,128)(2,1)S(1)}, bf16[128,512]{1,0:T(8,128)(2,1)S(1)}, u32[]{:S(2)}, u32[]{:S(2)}) %collective-permute-start.1) | collective-permute-done | bytes 131104 | tf_op jit(solution)/shard_map/ppermute | solution.py:24
  26.7 0.2 copy.55
  27.0 0.3 fusion.16
  27.5 0.3 fusion.6
  28.0 23.6 %all_to_all.29 = bf16[8,16,512]{2,1,0:T(8,128)(2,1)S(1)} all-to-all(bf16[8,16,512]{2,1,0:T(8,128)(2,1)S(1)} %all_to_all.22), channel_id=1, replica_groups=mesh['ctx'=128,'tp'=8] {'tp'}, dimensions={0} | all-to-all | bytes 262144 | tf_op jit(solution)/shard_map/all_to_all | solution.py:69
  51.7 0.9 copy-done
  52.5 0.2 multiply_reduce_fusion.1
  52.9 0.8 subtract_convert_fusion
  53.7 11.6 %all_to_all.30 = bf16[16,8,512]{2,0,1:T(8,128)(2,1)S(1)} all-to-all(bf16[16,8,512]{2,0,1:T(8,128)(2,1)S(1)} %bitcast.59), channel_id=1, replica_groups=mesh['ctx'=128,'tp'=8] {'tp'}, dimensions={1} | all-to-all | bytes 262144 | tf_op jit(solution)/shard_map/all_to_all | solution.py:78
  65.5 0.3 convolution_bitcast_fusion
  65.8 0.3 fusion.4
  66.2 0.3 fusion
  66.6 0.8 copy.74
  67.5 6.5 %collective-permute-start.4 = (f32[128,512]{0,1:T(8,128)}, f32[128,512]{0,1:T(8,128)S(1)}, u32[]{:S(2)}, u32[]{:S(2)}) collective-permute-start(f32[128,512]{0,1:T(8,128)} %bitcast.12), channel_id=1, source_target_pairs={{8,0},{16,8},{24,16},{32,24},{40,32},{48,40},{56,48},{64,56},{72,6... | collective-permute-start | bytes 786440 | tf_op jit(solution)/shard_map/ppermute | solution.py:34
  73.9 1.9 %collective-permute-start.5 = (f32[128,512]{0,1:T(8,128)S(1)}, f32[128,512]{0,1:T(8,128)S(1)}, u32[]{:S(2)}, u32[]{:S(2)}) collective-permute-start(f32[128,512]{0,1:T(8,128)S(1)} %bitcast.62), channel_id=1, source_target_pairs={{0,8},{8,16},{16,24},{24,32},{32,40},{40,48},{48,56},{56,64},{64,7... | collective-permute-start | bytes 786440 | tf_op jit(solution)/shard_map/ppermute | solution.py:34
  76.2 1.9 %collective-permute-start.7 = (f32[128,512]{1,0:T(8,128)S(1)}, f32[128,512]{1,0:T(8,128)S(1)}, u32[]{:S(2)}, u32[]{:S(2)}) collective-permute-start(f32[128,512]{1,0:T(8,128)S(1)} %copy.80), channel_id=1, source_target_pairs={{0,8},{8,16},{16,24},{24,32},{32,40},{40,48},{48,56},{56,64},{64,7... | collective-permute-start | bytes 786440 | tf_op jit(solution)/shard_map/ppermute | solution.py:34
  78.2 7.6 %collective-permute-start.6 = (f32[128,512]{1,0:T(8,128)S(1)}, f32[128,512]{1,0:T(8,128)S(1)}, u32[]{:S(2)}, u32[]{:S(2)}) collective-permute-start(f32[128,512]{1,0:T(8,128)S(1)} %copy.78), channel_id=1, source_target_pairs={{8,0},{16,8},{24,16},{32,24},{40,32},{48,40},{56,48},{64,56},{72,6... | collective-permute-start | bytes 786440 | tf_op jit(solution)/shard_map/ppermute | solution.py:34
  85.7 0.3 fusion.5
  86.0 0.8 copy.81
  87.1 0.6 collective-permute-done.5
  87.7 0.8 copy.82
  88.4 4.8 %collective-permute-done.7 = f32[128,512]{1,0:T(8,128)S(1)} collective-permute-done((f32[128,512]{1,0:T(8,128)S(1)}, f32[128,512]{1,0:T(8,128)S(1)}, u32[]{:S(2)}, u32[]{:S(2)}) %collective-permute-start.7) | collective-permute-done | bytes 262176 | tf_op jit(solution)/shard_map/ppermute | solution.py:34
  93.2 6.3 %collective-permute-done.6 = f32[128,512]{1,0:T(8,128)S(1)} collective-permute-done((f32[128,512]{1,0:T(8,128)S(1)}, f32[128,512]{1,0:T(8,128)S(1)}, u32[]{:S(2)}, u32[]{:S(2)}) %collective-permute-start.6) | collective-permute-done | bytes 262176 | tf_op jit(solution)/shard_map/ppermute | solution.py:34
  99.5 0.7 add_convert_fusion
  (35 shorter events, 1.9 us)
Async XLA Ops:
  0.6 11.6 %copy-start.2 = (bf16[128,512]{1,0:T(8,128)(2,1)S(1)}, bf16[128,512]{1,0:T(8,128)(2,1)}, u32[]{:S(2)}) copy-start(bf16[128,512]{1,0:T(8,128)(2,1)} %param.8) | copy-start | bytes 393220
  0.6 22.1 %copy-start.1 = (bf16[128,512]{1,0:T(8,128)(2,1)S(1)}, bf16[128,512]{1,0:T(8,128)(2,1)}, u32[]{:S(2)}) copy-start(bf16[128,512]{1,0:T(8,128)(2,1)} %param.6) | copy-start | bytes 393220
  1.7 25.2 %collective-permute-start.3 = (bf16[128,512]{0,1:T(8,128)(2,1)S(1)}, bf16[128,512]{0,1:T(8,128)(2,1)S(1)}, u32[]{:S(2)}, u32[]{:S(2)}) collective-permute-start(bf16[128,512]{0,1:T(8,128)(2,1)S(1)} %copy.56), channel_id=1, source_target_pairs={{8,0},{16,8},{24,16},{32,24},{40,32},{48,40},{56,48},{64,56},{72,6... | collective-permute-start | bytes 393224 | tf_op jit(solution)/shard_map/ppermute | solution.py:24
  10.3 16.6 %collective-permute-start.2 = (bf16[128,512]{0,1:T(8,128)(2,1)S(1)}, bf16[128,512]{0,1:T(8,128)(2,1)S(1)}, u32[]{:S(2)}, u32[]{:S(2)}) collective-permute-start(bf16[128,512]{0,1:T(8,128)(2,1)S(1)} %copy.56), channel_id=1, source_target_pairs={{0,8},{8,16},{16,24},{24,32},{32,40},{40,48},{48,56},{56,64},{64,7... | collective-permute-start | bytes 393224 | tf_op jit(solution)/shard_map/ppermute | solution.py:22
  12.2 11.6 %collective-permute-start = (bf16[128,512]{1,0:T(8,128)(2,1)S(1)}, bf16[128,512]{1,0:T(8,128)(2,1)S(1)}, u32[]{:S(2)}, u32[]{:S(2)}) collective-permute-start(bf16[128,512]{1,0:T(8,128)(2,1)S(1)} %copy-done.2), channel_id=1, source_target_pairs={{0,8},{8,16},{16,24},{24,32},{32,40},{40,48},{48,56},{56,64},{64,7... | collective-permute-start | bytes 393224 | tf_op jit(solution)/shard_map/ppermute | solution.py:22
  14.2 12.5 %collective-permute-start.1 = (bf16[128,512]{1,0:T(8,128)(2,1)S(1)}, bf16[128,512]{1,0:T(8,128)(2,1)S(1)}, u32[]{:S(2)}, u32[]{:S(2)}) collective-permute-start(bf16[128,512]{1,0:T(8,128)(2,1)S(1)} %copy-done.2), channel_id=1, source_target_pairs={{8,0},{16,8},{24,16},{32,24},{40,32},{48,40},{56,48},{64,56},{72,6... | collective-permute-start | bytes 393224 | tf_op jit(solution)/shard_map/ppermute | solution.py:24
  21.8 0.7 copy-start.4
  51.6 0.9 copy-start
  51.6 0.9 copy-start.3
  67.5 19.6 %collective-permute-start.4 = (f32[128,512]{0,1:T(8,128)}, f32[128,512]{0,1:T(8,128)S(1)}, u32[]{:S(2)}, u32[]{:S(2)}) collective-permute-start(f32[128,512]{0,1:T(8,128)} %bitcast.12), channel_id=1, source_target_pairs={{8,0},{16,8},{24,16},{32,24},{40,32},{48,40},{56,48},{64,56},{72,6... | collective-permute-start | bytes 786440 | tf_op jit(solution)/shard_map/ppermute | solution.py:34
  73.9 13.7 %collective-permute-start.5 = (f32[128,512]{0,1:T(8,128)S(1)}, f32[128,512]{0,1:T(8,128)S(1)}, u32[]{:S(2)}, u32[]{:S(2)}) collective-permute-start(f32[128,512]{0,1:T(8,128)S(1)} %bitcast.62), channel_id=1, source_target_pairs={{0,8},{8,16},{16,24},{24,32},{32,40},{40,48},{48,56},{56,64},{64,7... | collective-permute-start | bytes 786440 | tf_op jit(solution)/shard_map/ppermute | solution.py:34
  76.2 17.0 %collective-permute-start.7 = (f32[128,512]{1,0:T(8,128)S(1)}, f32[128,512]{1,0:T(8,128)S(1)}, u32[]{:S(2)}, u32[]{:S(2)}) collective-permute-start(f32[128,512]{1,0:T(8,128)S(1)} %copy.80), channel_id=1, source_target_pairs={{0,8},{8,16},{16,24},{24,32},{32,40},{40,48},{48,56},{56,64},{64,7... | collective-permute-start | bytes 786440 | tf_op jit(solution)/shard_map/ppermute | solution.py:34
  78.2 21.3 %collective-permute-start.6 = (f32[128,512]{1,0:T(8,128)S(1)}, f32[128,512]{1,0:T(8,128)S(1)}, u32[]{:S(2)}, u32[]{:S(2)}) collective-permute-start(f32[128,512]{1,0:T(8,128)S(1)} %copy.78), channel_id=1, source_target_pairs={{8,0},{16,8},{24,16},{32,24},{40,32},{48,40},{56,48},{64,56},{72,6... | collective-permute-start | bytes 786440 | tf_op jit(solution)/shard_map/ppermute | solution.py:34
where the time goes:
time: 101 us; the launch traced here: 100 us
  starting transfers between devices  37.9 us (38%)
  blocking collectives  35.2 us (35%)
  waiting for transfers between devices  15.5 us (15%)
  local copies, waits for them, and re-layouts  6.55 us (6%)
  other arithmetic  2.34 us (2%)
  matrix products  1.77 us (2%)
    all_to_all x1, blocking collectives, per_device(): lax.all_to_all(attended, 'tp', split_axis=0, concat_axis=1, tiled=True)  23.6 us
    ppermute x4, starting transfers between devices, passed_along(): return lax.ppermute(x, axis, pairs)  17.9 us
    ppermute x2, starting transfers between devices, with_halo(): lax.ppermute(head, axis, [((i + 1) % count, i) for i in range(ends)])  16.2 us
    ppermute x4, waiting for transfers between devices, passed_along(): return lax.ppermute(x, axis, pairs)  11.6 us
    all_to_all x1, blocking collectives, per_device(): lax.all_to_all(tile_grad, 'tp', split_axis=1, concat_axis=0, tiled=True)  11.6 us
    unnamed x13, local copies, waits for them, and re-layouts  4.16 us
    ppermute x2, starting transfers between devices, with_halo(): lax.ppermute(tail, axis, [(i, (i + 1) % count) for i in range(ends)])  3.84 us
    ppermute x2, waiting for transfers between devices, with_halo(): lax.ppermute(head, axis, [((i + 1) % count, i) for i in range(ends)])  2.89 us
  transfers between devices with their start and end apart: 8, of which 5 were waited for; matrix products, arithmetic and copies ran while one was open for 3% of the time, Pallas kernels for 0%

commit v1 on v0

v1 whole, which is shorter than its diff:
```python
import jax
import jax.numpy as jnp
from jax import lax
from jax.experimental import pallas as pl
from jax.experimental.pallas import tpu as pltpu
from jax.sharding import PartitionSpec as P

HSZ = 128
NEGATIVE = -1e30
EPSILON = 1e-06
MESH = pl.DeviceIdType.MESH
F32 = jnp.float32
BF16 = jnp.bfloat16


def dot_nn(a, b):
    return lax.dot_general(a, b, (((1,), (0,)), ((), ())), preferred_element_type=F32)


def dot_nt(a, b):
    return lax.dot_general(a, b, (((1,), (1,)), ((), ())), preferred_element_type=F32)


def dot_tn(a, b):
    return lax.dot_general(a, b, (((0,), (0,)), ((), ())), preferred_element_type=F32)


def columns_to_rows(columns):
    size = columns[0].shape[0]
    lane = lax.broadcasted_iota(jnp.int32, (size, size), 1)
    packed = jnp.zeros((size, size), F32)
    for i, column in enumerate(columns):
        packed = jnp.where(lane == i, column, packed)
    return jnp.transpose(packed)[0:8]


def rows_to_columns(rows):
    size = rows.shape[1]
    return jnp.transpose(jnp.concatenate([rows] * (size // 8), axis=0))


def make_kernel(blocks, peers, length, heads):
    width = heads * HSZ
    tile = length // peers
    model = width * peers
    scale = HSZ ** (-0.5)

    def kernel(
        q_hbm, k_hbm, v_hbm, mask_ref, gain_hbm, ng_hbm,
        normed_out, dq_out, dk_out, dv_out,
        q_own, k_own, v_own, q_p, k_p, v_p, q_r, k_r, v_r,
        gain, ng, probs, att, do_own, do_p, do_r,
        rows_own, rows_p, rows_r, stats, normed_v, dq_v, dk_v, dv_v,
        local_sem, out_sem, z_send, z_recv, r_send, r_recv,
        ng_send, ng_recv, st_send, st_recv, no_send, no_recv,
    ):
        b = lax.axis_index("ctx")
        t = lax.axis_index("tp")
        side = 1 - 2 * (b % 2)
        partner = b + side
        relay_to = (b + 2 * side + blocks) % blocks
        relay_from = (b - 2 * side + blocks) % blocks
        other = (b - side + blocks) % blocks

        barrier = pltpu.get_barrier_semaphore()
        greeted = [(partner, t), (relay_to, t), (relay_from, t)]
        greeted += [(b, (t + d) % peers) for d in range(1, peers)]
        for who in greeted:
            pl.semaphore_signal(barrier, inc=1, device_id=who, device_id_type=MESH)

        locals_ = []

        def local(src, dst):
            copy = pltpu.make_async_copy(src, dst, local_sem.at[len(locals_)])
            copy.start()
            locals_.append(copy)

        def cols(ref, h):
            return ref.at[:, pl.ds(h * HSZ, HSZ)]

        for h in range(heads):
            local(cols(k_hbm, h), k_own.at[h])
            local(cols(q_hbm, h), q_own.at[h])
            local(cols(v_hbm, h), v_own.at[h])
        local(ng_hbm.at[:, pl.ds(pl.multiple_of(t * width, width), width)],
              ng.at[pl.ds(pl.multiple_of(t * tile, tile), tile), :])
        local(gain_hbm.at[:, pl.ds(pl.multiple_of(t * width, width), width)], gain)

        pl.semaphore_wait(barrier, len(greeted))

        def remote(src, dst, send, recv, who):
            return pltpu.make_async_remote_copy(
                src_ref=src, dst_ref=dst, send_sem=send, recv_sem=recv,
                device_id=who, device_id_type=MESH)

        plan = []
        for h in range(heads):
            plan.append((cols(k_hbm, h), k_p.at[h], k_r.at[h]))
            plan.append((cols(v_hbm, h), v_p.at[h], v_r.at[h]))
        for h in range(heads):
            plan.append((cols(q_hbm, h), q_p.at[h], q_r.at[h]))
        for h in range(heads):
            plan.append((do_own.at[h], do_p.at[h], do_r.at[h]))
        plan.append((rows_own, rows_p, rows_r))
        to_partner = [
            remote(src, mid, z_send.at[i], z_recv.at[i], (partner, t))
            for i, (src, mid, _) in enumerate(plan)
        ]
        relayed = [
            remote(mid, end, r_send.at[i], r_recv.at[i], (relay_to, t))
            for i, (_, mid, end) in enumerate(plan)
        ]

        def pass_on(i):
            to_partner[i].wait_recv()
            relayed[i].start()

        first_q, first_do = 2 * heads, 3 * heads
        row_copy = 4 * heads
        for i in range(2 * heads):
            to_partner[i].start()

        ng_copies = []
        for d in range(1, peers):
            to = (t + d) % peers
            ng_copies.append(remote(
                ng_hbm.at[:, pl.ds(pl.multiple_of(to * width, width), width)],
                ng.at[pl.ds(pl.multiple_of(t * tile, tile), tile), :],
                ng_send.at[d - 1], ng_recv.at[d - 1], (b, to)))
        for copy in ng_copies:
            copy.start()
        for h in range(heads):
            to_partner[first_q + h].start()

        live_p = mask_ref[1 + side, b] > 0
        live_r = mask_ref[1 - side, b] > 0
        from_p = mask_ref[1 - side, partner] > 0
        from_r = mask_ref[1 + side, other] > 0

        for copy in locals_:
            copy.wait()

        lses = []

        def forward(h):
            query = q_own[h]
            own = dot_nt(query, k_own[h]) * scale
            near = jnp.where(live_p, dot_nt(query, k_p[h]) * scale, NEGATIVE)
            far = jnp.where(live_r, dot_nt(query, k_r[h]) * scale, NEGATIVE)
            peak = jnp.max(jnp.maximum(jnp.maximum(own, near), far), -1, keepdims=True)
            own, near, far = jnp.exp(own - peak), jnp.exp(near - peak), jnp.exp(far - peak)
            total = jnp.sum(own + near + far, -1, keepdims=True)
            inv = 1.0 / total
            lses.append(peak + jnp.log(total))
            own, near, far = own * inv, near * inv, far * inv
            probs[h, 0] = own
            probs[h, 1] = near
            probs[h, 2] = far
            out = (
                dot_nn(own.astype(BF16), v_own[h])
                + dot_nn(near.astype(BF16), v_p[h])
                + dot_nn(far.astype(BF16), v_r[h])
            )
            att[h] = out.astype(BF16)

        for h in range(heads):
            pass_on(2 * h)
            pass_on(2 * h + 1)
            if h > 0:
                relayed[2 * h - 2].wait_recv()
                relayed[2 * h - 1].wait_recv()
                forward(h - 1)
        relayed[2 * heads - 2].wait_recv()
        relayed[2 * heads - 1].wait_recv()
        forward(heads - 1)

        for copy in ng_copies:
            copy.wait_recv()

        def upstream(h):
            return ng[:, h * HSZ:(h + 1) * HSZ].astype(F32) * gain[:, h * HSZ:(h + 1) * HSZ]

        square = jnp.zeros((length, HSZ), F32)
        cross = jnp.zeros((length, HSZ), F32)
        for h in range(heads):
            value = att[h].astype(F32)
            square = square + value * value
            cross = cross + upstream(h) * value
        stats[t] = columns_to_rows(
            [jnp.sum(square, -1, keepdims=True), jnp.sum(cross, -1, keepdims=True)])
        st_copies = []
        for d in range(1, peers):
            to = (t + d) % peers
            st_copies.append(remote(
                stats.at[t], stats.at[t], st_send.at[d - 1], st_recv.at[d - 1], (b, to)))
        for copy in st_copies:
            copy.start()

        for h in range(heads):
            pass_on(first_q + h)

        for copy in st_copies:
            copy.wait_recv()
        sums = stats[0]
        for i in range(1, peers):
            sums = sums + stats[i]
        sums = rows_to_columns(sums)
        inverse = lax.rsqrt(sums[:, 0:1] / model + EPSILON)
        pull = inverse * inverse * inverse * (sums[:, 1:2] / model)

        deltas = []
        for h in range(heads):
            value = att[h].astype(F32)
            grad = (inverse * upstream(h) - value * pull).astype(BF16)
            do_own[h] = grad
            to_partner[first_do + h].start()
            deltas.append(jnp.sum(grad.astype(F32) * value, -1, keepdims=True))
        rows_own[...] = columns_to_rows(lses + deltas)
        to_partner[row_copy].start()
        for h in range(heads):
            value = att[h].astype(F32)
            normed_v[:, h * HSZ:(h + 1) * HSZ] = (
                value * inverse * gain[:, h * HSZ:(h + 1) * HSZ]).astype(BF16)
        no_copies = []
        for d in range(1, peers):
            to = (t + d) % peers
            no_copies.append(remote(
                normed_v.at[pl.ds(pl.multiple_of(to * tile, tile), tile), :],
                normed_out.at[:, pl.ds(pl.multiple_of(t * width, width), width)],
                no_send.at[d - 1], no_recv.at[d - 1], (b, to)))
        for copy in no_copies:
            copy.start()
        outs = []

        def store(src, dst):
            copy = pltpu.make_async_copy(src, dst, out_sem.at[len(outs)])
            copy.start()
            outs.append(copy)

        store(normed_v.at[pl.ds(pl.multiple_of(t * tile, tile), tile), :],
              normed_out.at[:, pl.ds(pl.multiple_of(t * width, width), width)])

        dks, dvs = [], []
        for h in range(heads):
            grad = do_own[h]
            ds = []
            for i, values in enumerate((v_own, v_p, v_r)):
                dp = dot_nt(grad, values[h])
                ds.append((probs[h, i] * (dp - deltas[h])).astype(BF16))
            dq = dot_nn(ds[0], k_own[h]) + dot_nn(ds[1], k_p[h]) + dot_nn(ds[2], k_r[h])
            dq_v[:, h * HSZ:(h + 1) * HSZ] = (dq * scale).astype(BF16)
            dk_v[h] = dot_tn(ds[0], q_own[h])
            dv_v[h] = dot_tn(probs[h, 0].astype(BF16), grad)
        store(dq_v, dq_out)

        for h in range(heads):
            pass_on(first_do + h)
        pass_on(row_copy)

        def key_side(h, queries, grads, rows, live):
            score = dot_nt(k_own[h], queries[h]) * scale
            prob = jnp.where(live, jnp.exp(score - rows[h:h + 1, :]), 0.0)
            grad = grads[h]
            dp = dot_nt(v_own[h], grad)
            ds = (prob * (dp - rows[heads + h:heads + h + 1, :])).astype(BF16)
            return dot_nn(ds, queries[h]), dot_nn(prob.astype(BF16), grad)

        for h in range(heads):
            dk, dv = key_side(h, q_p, do_p, rows_p, from_p)
            dk_v[h] += dk
            dv_v[h] += dv
        for h in range(heads):
            relayed[first_q + h].wait_recv()
        relayed[row_copy].wait_recv()
        for h in range(heads):
            relayed[first_do + h].wait_recv()
            dk, dv = key_side(h, q_r, do_r, rows_r, from_r)
            dks.append(((dk_v[h] + dk) * scale).astype(BF16))
            dvs.append((dv_v[h] + dv).astype(BF16))
        dk_b, dv_b = dq_v, normed_v
        for copy in outs:
            copy.wait()
        for copy in no_copies:
            copy.wait_send()
        for h in range(heads):
            dk_b[:, h * HSZ:(h + 1) * HSZ] = dks[h]
            dv_b[:, h * HSZ:(h + 1) * HSZ] = dvs[h]
        outs.clear()
        store(dk_b, dk_out)
        store(dv_b, dv_out)
        for copy in outs:
            copy.wait()
        for copy in no_copies:
            copy.wait_recv()
        for copy in to_partner + relayed + ng_copies + st_copies:
            copy.wait_send()

    return kernel


def attention(blocks, peers, queries, key_rows, value_rows, view_mask, norm_gain, normed_grad):
    length, width = queries.shape
    heads = width // HSZ
    tile, model = normed_grad.shape
    head_block = pltpu.VMEM((heads, length, HSZ), BF16)
    rows = pltpu.VMEM((8, length), F32)
    copies = 4 * heads + 1
    dma = pltpu.SemaphoreType.DMA
    any_ = pl.BlockSpec(memory_space=pltpu.HBM)
    flat = jax.ShapeDtypeStruct((length, width), BF16)
    return pl.pallas_call(
        make_kernel(blocks, peers, length, heads),
        out_shape=(jax.ShapeDtypeStruct((tile, model), BF16), flat, flat, flat),
        in_specs=[any_, any_, any_, pl.BlockSpec(memory_space=pltpu.SMEM), any_, any_],
        out_specs=(any_, any_, any_, any_),
        scratch_shapes=[head_block] * 9
        + [
            pltpu.VMEM((1, width), F32),
            pltpu.VMEM((length, width), BF16),
            pltpu.VMEM((heads, 3, length, length), F32),
        ]
        + [head_block] * 4
        + [rows] * 3
        + [
            pltpu.VMEM((peers, 8, length), F32),
            pltpu.VMEM((length, width), BF16),
            pltpu.VMEM((length, width), BF16),
            pltpu.VMEM((heads, length, HSZ), F32),
            pltpu.VMEM((heads, length, HSZ), F32),
            dma((3 * heads + 2,)),
            dma((4,)),
            dma((copies,)), dma((copies,)), dma((copies,)), dma((copies,)),
        ]
        + [dma((peers - 1,))] * 6,
        compiler_params=pltpu.CompilerParams(
            collective_id=0, has_side_effects=True, vmem_limit_bytes=60 * 1024 * 1024),
        cost_estimate=pl.CostEstimate(
            flops=2 * 22 * heads * length * length * HSZ,
            bytes_accessed=8 * length * width * 2,
            transcendentals=5 * heads * length * length),
    )(queries, key_rows, value_rows, view_mask.T, norm_gain.reshape(1, model), normed_grad)


def solution(mesh):
    blocks, peers = mesh.shape["ctx"], mesh.shape["tp"]

    def per_device(*arrays):
        return attention(blocks, peers, *arrays)

    placed = (P("ctx", "tp"), P("ctx", "tp"), P("ctx", "tp"), P(), P(), P(("ctx", "tp"), None))
    return jax.shard_map(
        per_device,
        mesh=mesh,
        in_specs=placed,
        out_specs=(P(("ctx", "tp"), None), P("ctx", "tp"), P("ctx", "tp"), P("ctx", "tp")),
        check_vma=False,
    )
```

time: 101 us -> 57.4 us (0.57)
  the two profiles are of different devices: /device:TPU:9 before, /device:TPU:1 now
where the time goes in v1:
time: 57.4 us; the launch traced here: 57.1 us
  Pallas kernels  52.3 us (91%)
  local copies, waits for them, and re-layouts  4.16 us (7%)
  between operations  0.65 us (1%)
    pallas_call x1, Pallas kernels, attention(): pl.pallas_call(make_kernel(blocks, peers, length, heads), out_shape=(jax....  52.3 us
    unnamed x10, local copies, waits for them, and re-layouts  4.16 us

profile of v1, /device:TPU:1, one launch (start us, length us, event | category | flops | bytes accessed | tf_op | source)
XLA Modules:
  0.0 57.1 jit_solution(1080298635237378736)
XLA Ops:
  0.6 52.3 %shard_map.93 = (bf16[16,4096]{1,0:T(8,128)(2,1)}, bf16[128,512]{1,0:T(8,128)(2,1)}, bf16[128,512]{1,0:T(8,128)(2,1)}, bf16[128,512]{1,0:T(8,128)(2,1)}) custom-call(bf16[128,512]{1,0:T(8,128)(2,1)} %q_hbm.1, bf16[128,512]{1,0:T(8,128)(2,1)} %k_hbm.1, bf16[128,512]{1,0:T(8,128)(2,1)} %v_hbm.1, s32[3,128]{1,0:T(4,128)} %bitcast.3, f32[1,4096]{1,0:T(1,128)} %bitcast.2, ...), custom_call_target="tpu_custom_call" | custom-call | flops 369098752 | bytes 1048576 | tf_op jit(solution)/shard_map/pallas_call | solution.py:311
  53.0 0.0 copy-start.2
  53.0 1.6 %copy.14 = bf16[16,4096]{1,0:T(8,128)(2,1)} copy(bf16[16,4096]{1,0:T(8,128)(2,1)} %get-tuple-element.8) | data formatting | bytes 262144
  54.6 0.0 copy-done.2
  54.6 0.0 copy-start.1
  54.6 0.7 %copy.15 = bf16[128,512]{1,0:T(8,128)(2,1)} copy(bf16[128,512]{1,0:T(8,128)(2,1)S(1)} %copy-done.2) | data formatting | bytes 262144
  55.2 0.3 copy-done.1
  55.5 0.0 copy-start
  55.5 0.7 %copy.16 = bf16[128,512]{1,0:T(8,128)(2,1)} copy(bf16[128,512]{1,0:T(8,128)(2,1)S(1)} %copy-done.1) | data formatting | bytes 262144
  56.2 0.3 copy-done
  56.5 0.7 %copy.17 = bf16[128,512]{1,0:T(8,128)(2,1)} copy(bf16[128,512]{1,0:T(8,128)(2,1)S(1)} %copy-done) | data formatting | bytes 262144
Async XLA Ops:
  53.0 1.6 %copy-start.2 = (bf16[128,512]{1,0:T(8,128)(2,1)S(1)}, bf16[128,512]{1,0:T(8,128)(2,1)}, u32[]{:S(2)}) copy-start(bf16[128,512]{1,0:T(8,128)(2,1)} %get-tuple-element.9) | copy-start | bytes 393220
  54.6 1.0 %copy-start.1 = (bf16[128,512]{1,0:T(8,128)(2,1)S(1)}, bf16[128,512]{1,0:T(8,128)(2,1)}, u32[]{:S(2)}) copy-start(bf16[128,512]{1,0:T(8,128)(2,1)} %get-tuple-element.10) | copy-start | bytes 393220
  55.5 1.0 %copy-start = (bf16[128,512]{1,0:T(8,128)(2,1)S(1)}, bf16[128,512]{1,0:T(8,128)(2,1)}, u32[]{:S(2)}) copy-start(bf16[128,512]{1,0:T(8,128)(2,1)} %get-tuple-element.11) | copy-start | bytes 393220

commit v2 on v1

v2 whole, which is shorter than its diff:
```python
import contextlib

import jax
import jax.numpy as jnp
from jax import lax
from jax.experimental import pallas as pl
from jax.experimental.pallas import tpu as pltpu
from jax.sharding import PartitionSpec as P

HSZ = 128
NEGATIVE = -1e30
EPSILON = 1e-06
MESH = pl.DeviceIdType.MESH
F32 = jnp.float32
BF16 = jnp.bfloat16
NG_AT = 0
Q_AT = 8
scope = contextlib.nullcontext


def dot_nn(a, b):
    return lax.dot_general(a, b, (((1,), (0,)), ((), ())), preferred_element_type=F32)


def dot_nt(a, b):
    return lax.dot_general(a, b, (((1,), (1,)), ((), ())), preferred_element_type=F32)


def dot_tn(a, b):
    return lax.dot_general(a, b, (((0,), (0,)), ((), ())), preferred_element_type=F32)


def columns_to_rows(columns):
    size = columns[0].shape[0]
    lane = lax.broadcasted_iota(jnp.int32, (size, size), 1)
    packed = jnp.zeros((size, size), F32)
    for i, column in enumerate(columns):
        packed = jnp.where(lane == i, column, packed)
    return jnp.transpose(packed)[0:8]


def rows_to_columns(rows):
    size = rows.shape[1]
    return jnp.transpose(jnp.concatenate([rows] * (size // 8), axis=0))


def make_kernel(blocks, peers, length, heads):
    width = heads * HSZ
    tile = length // peers
    model = width * peers
    half = heads // 2
    scale = HSZ ** (-0.5)

    def kernel(
        q_hbm, k_hbm, v_hbm, mask_ref, gain_hbm, ng_hbm,
        normed_out, dq_out, dk_out, dv_out,
        q_own, k_own, v_own, att, do_own, q_p, k_p, v_p, do_p, q_r, k_r, v_r, do_r,
        ng, gain, probs, far_probs, tiles, normed_v, spread,
        lse_own, lse_p, lse_r, row_own, row_p, row_r, stats, dq_v, dk_v, dv_v, dk_f, dv_f,
        local_sem, out_sem, z_send, z_recv, r_send, r_recv, row_send, row_recv,
        ng_send, ng_recv, st_send, st_recv, at_send, at_recv,
    ):
        b = lax.axis_index("ctx")
        t = lax.axis_index("tp")
        side = 1 - 2 * (b % 2)
        partner = b + side
        relay_to = (b + 2 * side + blocks) % blocks
        relay_from = (b - 2 * side + blocks) % blocks
        other = (b - side + blocks) % blocks

        barrier = pltpu.get_barrier_semaphore()
        greeted = [(partner, t), (relay_to, t), (relay_from, t), (other, t)]
        greeted += [(b, (t + d) % peers) for d in range(1, peers)]
        for who in greeted:
            pl.semaphore_signal(barrier, inc=1, device_id=who, device_id_type=MESH)

        locals_ = []

        def local(src, dst):
            copy = pltpu.make_async_copy(src, dst, local_sem.at[len(locals_)])
            copy.start()
            locals_.append(copy)

        def cols(ref, h):
            return ref.at[:, pl.ds(h * HSZ, HSZ)]

        def part(h):
            return slice(h * HSZ, (h + 1) * HSZ)

        my_cols = pl.ds(pl.multiple_of(t * width, width), width)
        my_rows = pl.ds(pl.multiple_of(t * tile, tile), tile)

        for h in range(heads):
            local(cols(k_hbm, h), k_own.at[h])
            local(cols(q_hbm, h), q_own.at[h])
            local(cols(v_hbm, h), v_own.at[h])
        local(ng_hbm.at[:, my_cols], ng.at[my_rows, :])
        local(gain_hbm, gain)

        with scope("barrier_wait"):
            pl.semaphore_wait(barrier, len(greeted))

        def remote(src, dst, send, recv, who):
            return pltpu.make_async_remote_copy(
                src_ref=src, dst_ref=dst, send_sem=send, recv_sem=recv,
                device_id=who, device_id_type=MESH)

        plan = []
        for h in range(heads):
            plan.append((cols(k_hbm, h), k_p.at[h], k_r.at[h]))
            plan.append((cols(v_hbm, h), v_p.at[h], v_r.at[h]))
        for h in range(0, heads, half):
            plan.append(tuple(x.at[pl.ds(h, half)] for x in (q_own, q_p, q_r)))
        for h in range(heads):
            plan.append((do_own.at[h], do_p.at[h], do_r.at[h]))
        to_partner = [
            remote(src, mid, z_send.at[i], z_recv.at[i], (partner, t))
            for i, (src, mid, _) in enumerate(plan)
        ]
        relayed = [
            remote(mid, end, r_send.at[i], r_recv.at[i], (relay_to, t))
            for i, (_, mid, end) in enumerate(plan)
        ]
        kvs = range(2 * heads)
        qs = range(2 * heads, 2 * heads + 2)
        dos = range(2 * heads + 2, 3 * heads + 2)

        def pass_on(i):
            with scope(f"pass_on{i}"):
                to_partner[i].wait_recv()
                relayed[i].start()

        def peer_copies(source, target, send, recv):
            copies = []
            for d in range(1, peers):
                to = (t + d) % peers
                copies.append(remote(source(to), target, send.at[d - 1], recv.at[d - 1], (b, to)))
            return copies

        ng_copies = peer_copies(
            lambda to: ng_hbm.at[:, pl.ds(pl.multiple_of(to * width, width), width)],
            ng.at[my_rows, :], ng_send, ng_recv)
        st_copies = peer_copies(lambda to: stats.at[t, pl.ds(0, 2)], stats.at[t, pl.ds(0, 2)], st_send, st_recv)
        at_copies = peer_copies(
            lambda to: att.at[:, pl.ds(pl.multiple_of(to * tile, tile), tile), :],
            tiles.at[t], at_send, at_recv)
        lse_copies = [
            remote(lse_own, lse_p, row_send.at[0], row_recv.at[0], (partner, t)),
            remote(lse_own, lse_r, row_send.at[1], row_recv.at[1], (other, t)),
        ]
        row_copies = [
            remote(row_own, row_p, row_send.at[2], row_recv.at[2], (partner, t)),
            remote(row_own, row_r, row_send.at[3], row_recv.at[3], (other, t)),
        ]

        def start(copies):
            for copy in copies:
                copy.start()

        for i in kvs:
            to_partner[i].start()
        if NG_AT == 0:
            start(ng_copies)

        live_p = mask_ref[1 + side, b] > 0
        live_r = mask_ref[1 - side, b] > 0
        from_p = mask_ref[1 - side, partner] > 0
        from_r = mask_ref[1 + side, other] > 0

        with scope("locals"):
            for copy in locals_:
                copy.wait()
        for i in kvs:
            pass_on(i)
            if i + 1 == NG_AT:
                start(ng_copies)
            if i + 1 == Q_AT:
                start([to_partner[j] for j in qs])

        lses = []

        def forward(h):
            query = q_own[h]
            own = dot_nt(query, k_own[h]) * scale
            near = jnp.where(live_p, dot_nt(query, k_p[h]) * scale, NEGATIVE)
            far = jnp.where(live_r, dot_nt(query, k_r[h]) * scale, NEGATIVE)
            peak = jnp.max(jnp.maximum(jnp.maximum(own, near), far), -1, keepdims=True)
            own, near, far = jnp.exp(own - peak), jnp.exp(near - peak), jnp.exp(far - peak)
            total = jnp.sum(own + near + far, -1, keepdims=True)
            inv = 1.0 / total
            lses.append(peak + jnp.log(total))
            own, near, far = own * inv, near * inv, far * inv
            probs[h, 0] = own
            probs[h, 1] = near
            probs[h, 2] = far
            out = (
                dot_nn(own.astype(BF16), v_own[h])
                + dot_nn(near.astype(BF16), v_p[h])
                + dot_nn(far.astype(BF16), v_r[h])
            )
            att[h] = out.astype(BF16)

        for h in range(heads):
            with scope(f"wait_kv{h}"):
                relayed[2 * h].wait_recv()
                relayed[2 * h + 1].wait_recv()
            with scope(f"forward{h}"):
                forward(h)

        my_gain = [gain[:, pl.ds(pl.multiple_of(t * width + h * HSZ, HSZ), HSZ)] for h in range(heads)]

        with scope("wait_ng"):
            for copy in ng_copies:
                copy.wait_recv()
        square = jnp.zeros((length, HSZ), F32)
        cross = jnp.zeros((length, HSZ), F32)
        for h in range(heads):
            value = att[h].astype(F32)
            square = square + value * value
            cross = cross + ng[:, part(h)].astype(F32) * my_gain[h] * value
        stats[t] = columns_to_rows(
            [jnp.sum(square, -1, keepdims=True), jnp.sum(cross, -1, keepdims=True)])
        start(st_copies)
        lse_own[...] = columns_to_rows(lses)
        start(lse_copies)
        if Q_AT > 2 * heads:
            start([to_partner[i] for i in qs])
        start(at_copies)

        for i in qs:
            pass_on(i)

        def key_probs(side_index, queries, rows, live):
            for h in range(heads):
                score = dot_nt(k_own[h], queries[h]) * scale
                far_probs[side_index, h] = jnp.where(live, jnp.exp(score - rows[h:h + 1, :]), 0.0)

        with scope("probs_p"):
            lse_copies[0].wait_recv()
            key_probs(0, q_p, lse_p, from_p)
        with scope("wait_stats"):
            for copy in st_copies:
                copy.wait_recv()
        sums = stats[0]
        for i in range(1, peers):
            sums = sums + stats[i]
        sums = rows_to_columns(sums)
        inverse = lax.rsqrt(sums[:, 0:1] / model + EPSILON)
        pull = inverse * inverse * inverse * (sums[:, 1:2] / model)

        with scope("gradient"):
            deltas = []
            for h in range(heads):
                value = att[h].astype(F32)
                up = ng[:, part(h)].astype(F32) * my_gain[h]
                grad = (inverse * up - value * pull).astype(BF16)
                do_own[h] = grad
                deltas.append(jnp.sum(grad.astype(F32) * value, -1, keepdims=True))
            row_own[...] = columns_to_rows(deltas)
            start(row_copies)
            start([to_partner[i] for i in dos])

        outs = []

        def store(src, dst):
            copy = pltpu.make_async_copy(src, dst, out_sem.at[len(outs)])
            copy.start()
            outs.append(copy)

        for h in range(heads):
            with scope(f"own{h}"):
                grad = do_own[h]
                ds = []
                for i, values in enumerate((v_own, v_p, v_r)):
                    dp = dot_nt(grad, values[h])
                    ds.append((probs[h, i] * (dp - deltas[h])).astype(BF16))
                dq = dot_nn(ds[0], k_own[h]) + dot_nn(ds[1], k_p[h]) + dot_nn(ds[2], k_r[h])
                dq_v[:, part(h)] = (dq * scale).astype(BF16)
                dk_f[h] = dot_tn(ds[0], q_own[h])
                dv_f[h] = dot_tn(probs[h, 0].astype(BF16), grad)
        store(dq_v, dq_out)

        def key_side(h, index, queries, grads, rows):
            grad = grads[h]
            prob = far_probs[index, h]
            dp = dot_nt(v_own[h], grad)
            ds = (prob * (dp - rows[h:h + 1, :])).astype(BF16)
            return dot_nn(ds, queries[h]), dot_nn(prob.astype(BF16), grad)

        with scope("probs_r"):
            lse_copies[1].wait_recv()
            for i in qs:
                relayed[i].wait_recv()
            key_probs(1, q_r, lse_r, from_r)

        for i in dos:
            pass_on(i)
        with scope("wait_row_p"):
            row_copies[0].wait_recv()
        for h in range(heads):
            with scope(f"key_p{h}"):
                dk, dv = key_side(h, 0, q_p, do_p, row_p)
                dk_f[h] += dk
                dv_f[h] += dv

        with scope("wait_tiles"):
            for copy in at_copies:
                copy.wait_recv()
        with scope("normed"):
            tiles[t] = att[:, my_rows, :]
            spread[...] = jnp.broadcast_to(inverse, (length, HSZ))
            tile_inverse = spread[my_rows, :]
            for p in range(peers):
                for h in range(heads):
                    c = p * heads + h
                    normed_v[:, part(c)] = (
                        tiles[p, h].astype(F32) * tile_inverse * gain[:, part(c)]).astype(BF16)
            store(normed_v, normed_out)

        with scope("wait_row_r"):
            row_copies[1].wait_recv()
        for h in range(heads):
            with scope(f"wait_do{h}"):
                relayed[dos[h]].wait_recv()
            with scope(f"key_r{h}"):
                dk, dv = key_side(h, 1, q_r, do_r, row_r)
                dk_v[:, part(h)] = ((dk_f[h] + dk) * scale).astype(BF16)
                dv_v[:, part(h)] = (dv_f[h] + dv).astype(BF16)
                if h % 2 == 1:
                    both = slice((h - 1) * HSZ, (h + 1) * HSZ)
                    store(dk_v.at[:, both], dk_out.at[:, both])
                    store(dv_v.at[:, both], dv_out.at[:, both])
        with scope("wait_sends"):
            for copy in to_partner + relayed + ng_copies + st_copies + at_copies + lse_copies + row_copies:
                copy.wait_send()
        with scope("wait_outs"):
            for copy in outs:
                copy.wait()

    return kernel


def attention(blocks, peers, queries, key_rows, value_rows, view_mask, norm_gain, normed_grad):
    length, width = queries.shape
    heads = width // HSZ
    tile, model = normed_grad.shape
    head_block = pltpu.VMEM((heads, length, HSZ), BF16)
    flat_block = pltpu.VMEM((length, width), BF16)
    total_block = pltpu.VMEM((heads, length, HSZ), F32)
    rows = pltpu.VMEM((8, length), F32)
    copies = 3 * heads + 2
    dma = pltpu.SemaphoreType.DMA
    any_ = pl.BlockSpec(memory_space=pl.ANY)
    flat = jax.ShapeDtypeStruct((length, width), BF16)
    return pl.pallas_call(
        make_kernel(blocks, peers, length, heads),
        out_shape=(jax.ShapeDtypeStruct((tile, model), BF16), flat, flat, flat),
        in_specs=[any_, any_, any_, pl.BlockSpec(memory_space=pltpu.SMEM), any_, any_],
        out_specs=(any_, any_, any_, any_),
        scratch_shapes=[head_block] * 13
        + [flat_block]
        + [
            pltpu.VMEM((1, model), F32),
            pltpu.VMEM((heads, 3, length, length), F32),
            pltpu.VMEM((2, heads, length, length), F32),
            pltpu.VMEM((peers, heads, tile, HSZ), BF16),
            pltpu.VMEM((tile, model), BF16),
            pltpu.VMEM((length, HSZ), F32),
        ]
        + [rows] * 6
        + [pltpu.VMEM((peers, 8, length), F32)]
        + [flat_block] * 3
        + [total_block] * 2
        + [
            dma((3 * heads + 2,)),
            dma((heads + 2,)),
            dma((copies,)), dma((copies,)), dma((copies,)), dma((copies,)),
            dma((4,)), dma((4,)),
        ]
        + [dma((peers - 1,))] * 6,
        compiler_params=pltpu.CompilerParams(
            collective_id=0, has_side_effects=True, vmem_limit_bytes=60 * 1024 * 1024),
        cost_estimate=pl.CostEstimate(
            flops=2 * 22 * heads * length * length * HSZ,
            bytes_accessed=8 * length * width * 2,
            transcendentals=5 * heads * length * length),
    )(queries, key_rows, value_rows, view_mask.T, norm_gain.reshape(1, model), normed_grad)


def copy_out(*arrays):
    n = len(arrays)

    def kernel(*refs):
        sources, outs, held, sems = refs[:n], refs[n:2 * n], refs[2 * n:3 * n], refs[3 * n]
        loads = [pltpu.make_async_copy(sources[i], held[i], sems.at[i]) for i in range(n)]
        stores = [pltpu.make_async_copy(held[i], outs[i], sems.at[n + i]) for i in range(n)]
        for copy in loads:
            copy.start()
        for load, copy in zip(loads, stores):
            load.wait()
            copy.start()
        for copy in stores:
            copy.wait()

    any_ = pl.BlockSpec(memory_space=pl.ANY)
    return pl.pallas_call(
        kernel,
        out_shape=tuple(jax.ShapeDtypeStruct(x.shape, x.dtype) for x in arrays),
        in_specs=[any_] * n,
        out_specs=(any_,) * n,
        scratch_shapes=[pltpu.VMEM(x.shape, x.dtype) for x in arrays]
        + [pltpu.SemaphoreType.DMA((2 * n,))],
        compiler_params=pltpu.CompilerParams(vmem_limit_bytes=60 * 1024 * 1024),
    )(*arrays)


def solution(mesh):
    blocks, peers = mesh.shape["ctx"], mesh.shape["tp"]

    def per_device(*arrays):
        return copy_out(*attention(blocks, peers, *arrays))

    placed = (P("ctx", "tp"), P("ctx", "tp"), P("ctx", "tp"), P(), P(), P(("ctx", "tp"), None))
    return jax.shard_map(
        per_device,
        mesh=mesh,
        in_specs=placed,
        out_specs=(P(("ctx", "tp"), None), P("ctx", "tp"), P("ctx", "tp"), P("ctx", "tp")),
        check_vma=False,
    )
```

time: 57.4 us -> 54.6 us (0.951)
  local copies, waits for them, and re-layouts: 4.16 us -> 0 us
  Pallas kernels: 52.3 us -> 53.7 us
    unnamed x10 -> x0, local copies, waits for them, and re-layouts: 4.16 us -> none
    pallas_call x0 -> x1, Pallas kernels: none -> 1.82 us  [copy_out(): pl.pallas_call(kernel, out_shape=tuple((jax.ShapeDtypeStruct(x.shape, x.d...]
where the time goes in v2:
time: 54.6 us; the launch traced here: 54.4 us
  Pallas kernels  53.7 us (98%)
  between operations  0.64 us (1%)
    pallas_call x1, Pallas kernels, attention(): pl.pallas_call(make_kernel(blocks, peers, length, heads), out_shape=(jax....  51.9 us
    pallas_call x1, Pallas kernels, copy_out(): pl.pallas_call(kernel, out_shape=tuple((jax.ShapeDtypeStruct(x.shape, x.d...  1.82 us

profile of v2, /device:TPU:1, one launch (start us, length us, event | category | flops | bytes accessed | tf_op | source)
XLA Modules:
  0.0 54.4 jit_solution(14486473043988334679)
XLA Ops:
  0.6 51.9 %shard_map.93 = (bf16[16,4096]{1,0:T(8,128)(2,1)}, bf16[128,512]{1,0:T(8,128)(2,1)}, bf16[128,512]{1,0:T(8,128)(2,1)}, bf16[128,512]{1,0:T(8,128)(2,1)}) custom-call(bf16[128,512]{1,0:T(8,128)(2,1)} %q_hbm.1, bf16[128,512]{1,0:T(8,128)(2,1)} %k_hbm.1, bf16[128,512]{1,0:T(8,128)(2,1)} %v_hbm.1, s32[3,128]{1,0:T(4,128)} %bitcast.3, f32[1,4096]{1,0:T(1,128)} %bitcast.2, ...), custom_call_target="tpu_custom_call" | custom-call | flops 369098752 | bytes 1048576 | tf_op jit(solution)/shard_map/pallas_call | solution.py:355
  52.6 1.8 %shard_map.94 = (bf16[16,4096]{1,0:T(8,128)(2,1)}, bf16[128,512]{1,0:T(8,128)(2,1)}, bf16[128,512]{1,0:T(8,128)(2,1)}, bf16[128,512]{1,0:T(8,128)(2,1)}) custom-call(bf16[16,4096]{1,0:T(8,128)(2,1)} %get-tuple-element.8.refs_0_, bf16[128,512]{1,0:T(8,128)(2,1)} %get-tuple-element.9.refs_1_, bf16[128,512]{1,0:T(8,128)(2,1)} %get-tuple-element.10.refs_2_, ...), custom_call_target="tpu_custom_call" | custom-call | tf_op jit(solution)/shard_map/pallas_call | solution.py:406

commit v3 on v2

--- a/solution.py
+++ b/solution.py
@@ -13,8 +13,6 @@
 MESH = pl.DeviceIdType.MESH
 F32 = jnp.float32
 BF16 = jnp.bfloat16
-NG_AT = 0
-Q_AT = 8
 scope = contextlib.nullcontext
 
 
@@ -44,6 +42,20 @@
     return jnp.transpose(jnp.concatenate([rows] * (size // 8), axis=0))
 
 
+class Edge:
+    def __init__(self, copy, sends, receives):
+        self.copy, self.sends, self.receives = copy, sends, receives
+
+    def start(self):
+        pl.when(self.sends)(self.copy.start)
+
+    def wait_send(self):
+        pl.when(self.sends)(self.copy.wait_send)
+
+    def wait_recv(self):
+        pl.when(self.receives)(self.copy.wait_recv)
+
+
 def make_kernel(blocks, peers, length, heads):
     width = heads * HSZ
     tile = length // peers
@@ -55,9 +67,9 @@
         q_hbm, k_hbm, v_hbm, mask_ref, gain_hbm, ng_hbm,
         normed_out, dq_out, dk_out, dv_out,
         q_own, k_own, v_own, att, do_own, q_p, k_p, v_p, do_p, q_r, k_r, v_r, do_r,
-        ng, gain, probs, far_probs, tiles, normed_v, spread,
-        lse_own, lse_p, lse_r, row_own, row_p, row_r, stats, dq_v, dk_v, dv_v, dk_f, dv_f,
-        local_sem, out_sem, z_send, z_recv, r_send, r_recv, row_send, row_recv,
+        ng, gain, probs, far_probs, tiles, spread,
+        lse_own, lse_p, lse_r, row_own, row_p, row_r, stats, dk_f, dv_f,
+        local_sem, z_send, z_recv, r_send, r_recv, row_send, row_recv,
         ng_send, ng_recv, st_send, st_recv, at_send, at_recv,
     ):
         b = lax.axis_index("ctx")
@@ -68,11 +80,30 @@
         relay_from = (b - 2 * side + blocks) % blocks
         other = (b - side + blocks) % blocks
 
+        even = side > 0
+        has_far = jnp.where(even, b > 0, b < blocks - 1)
+        has_next = jnp.where(even, b < blocks - 2, b > 1)
+
         barrier = pltpu.get_barrier_semaphore()
-        greeted = [(partner, t), (relay_to, t), (relay_from, t), (other, t)]
-        greeted += [(b, (t + d) % peers) for d in range(1, peers)]
-        for who in greeted:
+
+        def greet(who):
             pl.semaphore_signal(barrier, inc=1, device_id=who, device_id_type=MESH)
+
+        greet((partner, t))
+
+        @pl.when(has_next)
+        def _():
+            greet((relay_to, t))
+
+        @pl.when(has_far)
+        def _():
+            greet((relay_from, t))
+            greet((other, t))
+
+        for d in range(peers // 2, 0, -1):
+            greet((b, (t + d) % peers))
+            if 2 * d != peers:
+                greet((b, (t + peers - d) % peers))
 
         locals_ = []
 
@@ -90,15 +121,9 @@
         my_cols = pl.ds(pl.multiple_of(t * width, width), width)
         my_rows = pl.ds(pl.multiple_of(t * tile, tile), tile)
 
-        for h in range(heads):
-            local(cols(k_hbm, h), k_own.at[h])
-            local(cols(q_hbm, h), q_own.at[h])
-            local(cols(v_hbm, h), v_own.at[h])
-        local(ng_hbm.at[:, my_cols], ng.at[my_rows, :])
-        local(gain_hbm, gain)
-
         with scope("barrier_wait"):
-            pl.semaphore_wait(barrier, len(greeted))
+            pl.semaphore_wait(
+                barrier, peers + jnp.where(has_next, 1, 0) + jnp.where(has_far, 2, 0))
 
         def remote(src, dst, send, recv, who):
             return pltpu.make_async_remote_copy(
@@ -108,6 +133,7 @@
         plan = []
         for h in range(heads):
             plan.append((cols(k_hbm, h), k_p.at[h], k_r.at[h]))
+        for h in range(heads):
             plan.append((cols(v_hbm, h), v_p.at[h], v_r.at[h]))
         for h in range(0, heads, half):
             plan.append(tuple(x.at[pl.ds(h, half)] for x in (q_own, q_p, q_r)))
@@ -118,7 +144,7 @@
             for i, (src, mid, _) in enumerate(plan)
         ]
         relayed = [
-            remote(mid, end, r_send.at[i], r_recv.at[i], (relay_to, t))
+            Edge(remote(mid, end, r_send.at[i], r_recv.at[i], (relay_to, t)), has_next, has_far)
             for i, (_, mid, end) in enumerate(plan)
         ]
         kvs = range(2 * heads)
@@ -130,9 +156,11 @@
                 to_partner[i].wait_recv()
                 relayed[i].start()
 
+        farthest_first = sorted(range(1, peers), key=lambda d: -min(d, peers - d))
+
         def peer_copies(source, target, send, recv):
             copies = []
-            for d in range(1, peers):
+            for d in farthest_first:
                 to = (t + d) % peers
                 copies.append(remote(source(to), target, send.at[d - 1], recv.at[d - 1], (b, to)))
             return copies
@@ -146,11 +174,11 @@
             tiles.at[t], at_send, at_recv)
         lse_copies = [
             remote(lse_own, lse_p, row_send.at[0], row_recv.at[0], (partner, t)),
-            remote(lse_own, lse_r, row_send.at[1], row_recv.at[1], (other, t)),
+            Edge(remote(lse_own, lse_r, row_send.at[1], row_recv.at[1], (other, t)), has_far, has_far),
         ]
         row_copies = [
             remote(row_own, row_p, row_send.at[2], row_recv.at[2], (partner, t)),
-            remote(row_own, row_r, row_send.at[3], row_recv.at[3], (other, t)),
+            Edge(remote(row_own, row_r, row_send.at[3], row_recv.at[3], (other, t)), has_far, has_far),
         ]
 
         def start(copies):
@@ -159,8 +187,19 @@
 
         for i in kvs:
             to_partner[i].start()
-        if NG_AT == 0:
-            start(ng_copies)
+        start(ng_copies)
+
+        for h in range(heads):
+            local(cols(k_hbm, h), k_own.at[h])
+            local(cols(q_hbm, h), q_own.at[h])
+            local(cols(v_hbm, h), v_own.at[h])
+        local(ng_hbm.at[:, my_cols], ng.at[my_rows, :])
+        local(gain_hbm, gain)
+
+        @pl.when(jnp.logical_not(has_far))
+        def _():
+            for ref in (q_r, k_r, v_r, do_r, lse_r, row_r):
+                ref[...] = jnp.zeros_like(ref)
 
         live_p = mask_ref[1 + side, b] > 0
         live_r = mask_ref[1 - side, b] > 0
@@ -172,10 +211,7 @@
                 copy.wait()
         for i in kvs:
             pass_on(i)
-            if i + 1 == NG_AT:
-                start(ng_copies)
-            if i + 1 == Q_AT:
-                start([to_partner[j] for j in qs])
+        start([to_partner[i] for i in qs])
 
         lses = []
 
@@ -193,19 +229,19 @@
             probs[h, 0] = own
             probs[h, 1] = near
             probs[h, 2] = far
-            out = (
-                dot_nn(own.astype(BF16), v_own[h])
-                + dot_nn(near.astype(BF16), v_p[h])
-                + dot_nn(far.astype(BF16), v_r[h])
-            )
-            att[h] = out.astype(BF16)
-
-        for h in range(heads):
-            with scope(f"wait_kv{h}"):
-                relayed[2 * h].wait_recv()
-                relayed[2 * h + 1].wait_recv()
+            dk_f[h] = dot_nn(own.astype(BF16), v_own[h]) + dot_nn(near.astype(BF16), v_p[h])
+
+        for h in range(heads):
+            with scope(f"wait_k{h}"):
+                relayed[h].wait_recv()
             with scope(f"forward{h}"):
                 forward(h)
+        for h in range(heads):
+            with scope(f"wait_v{h}"):
+                relayed[heads + h].wait_recv()
+            with scope(f"attend{h}"):
+                out = dk_f[h] + dot_nn(probs[h, 2].astype(BF16), v_r[h])
+                att[h] = out.astype(BF16)
 
         my_gain = [gain[:, pl.ds(pl.multiple_of(t * width + h * HSZ, HSZ), HSZ)] for h in range(heads)]
 
@@ -223,8 +259,6 @@
         start(st_copies)
         lse_own[...] = columns_to_rows(lses)
         start(lse_copies)
-        if Q_AT > 2 * heads:
-            start([to_partner[i] for i in qs])
         start(at_copies)
 
         for i in qs:
@@ -260,13 +294,6 @@
             start(row_copies)
             start([to_partner[i] for i in dos])
 
-        outs = []
-
-        def store(src, dst):
-            copy = pltpu.make_async_copy(src, dst, out_sem.at[len(outs)])
-            copy.start()
-            outs.append(copy)
-
         for h in range(heads):
             with scope(f"own{h}"):
                 grad = do_own[h]
@@ -275,10 +302,9 @@
                     dp = dot_nt(grad, values[h])
                     ds.append((probs[h, i] * (dp - deltas[h])).astype(BF16))
                 dq = dot_nn(ds[0], k_own[h]) + dot_nn(ds[1], k_p[h]) + dot_nn(ds[2], k_r[h])
-                dq_v[:, part(h)] = (dq * scale).astype(BF16)
+                dq_out[:, part(h)] = (dq * scale).astype(BF16)
                 dk_f[h] = dot_tn(ds[0], q_own[h])
                 dv_f[h] = dot_tn(probs[h, 0].astype(BF16), grad)
-        store(dq_v, dq_out)
 
         def key_side(h, index, queries, grads, rows):
             grad = grads[h]
@@ -313,9 +339,8 @@
             for p in range(peers):
                 for h in range(heads):
                     c = p * heads + h
-                    normed_v[:, part(c)] = (
+                    normed_out[:, part(c)] = (
                         tiles[p, h].astype(F32) * tile_inverse * gain[:, part(c)]).astype(BF16)
-            store(normed_v, normed_out)
 
         with scope("wait_row_r"):
             row_copies[1].wait_recv()
@@ -324,18 +349,11 @@
                 relayed[dos[h]].wait_recv()
             with scope(f"key_r{h}"):
                 dk, dv = key_side(h, 1, q_r, do_r, row_r)
-                dk_v[:, part(h)] = ((dk_f[h] + dk) * scale).astype(BF16)
-                dv_v[:, part(h)] = (dv_f[h] + dv).astype(BF16)
-                if h % 2 == 1:
-                    both = slice((h - 1) * HSZ, (h + 1) * HSZ)
-                    store(dk_v.at[:, both], dk_out.at[:, both])
-                    store(dv_v.at[:, both], dv_out.at[:, both])
+                dk_out[:, part(h)] = ((dk_f[h] + dk) * scale).astype(BF16)
+                dv_out[:, part(h)] = (dv_f[h] + dv).astype(BF16)
         with scope("wait_sends"):
             for copy in to_partner + relayed + ng_copies + st_copies + at_copies + lse_copies + row_copies:
                 copy.wait_send()
-        with scope("wait_outs"):
-            for copy in outs:
-                copy.wait()
 
     return kernel
 
@@ -356,7 +374,7 @@
         make_kernel(blocks, peers, length, heads),
         out_shape=(jax.ShapeDtypeStruct((tile, model), BF16), flat, flat, flat),
         in_specs=[any_, any_, any_, pl.BlockSpec(memory_space=pltpu.SMEM), any_, any_],
-        out_specs=(any_, any_, any_, any_),
+        out_specs=(pl.BlockSpec(memory_space=pltpu.VMEM),) * 4,
         scratch_shapes=[head_block] * 13
         + [flat_block]
         + [
@@ -364,22 +382,19 @@
             pltpu.VMEM((heads, 3, length, length), F32),
             pltpu.VMEM((2, heads, length, length), F32),
             pltpu.VMEM((peers, heads, tile, HSZ), BF16),
-            pltpu.VMEM((tile, model), BF16),
             pltpu.VMEM((length, HSZ), F32),
         ]
         + [rows] * 6
         + [pltpu.VMEM((peers, 8, length), F32)]
-        + [flat_block] * 3
         + [total_block] * 2
         + [
             dma((3 * heads + 2,)),
-            dma((heads + 2,)),
             dma((copies,)), dma((copies,)), dma((copies,)), dma((copies,)),
             dma((4,)), dma((4,)),
         ]
         + [dma((peers - 1,))] * 6,
         compiler_params=pltpu.CompilerParams(
-            collective_id=0, has_side_effects=True, vmem_limit_bytes=60 * 1024 * 1024),
+            collective_id=0, has_side_effects=True, vmem_limit_bytes=55990000),
         cost_estimate=pl.CostEstimate(
             flops=2 * 22 * heads * length * length * HSZ,
             bytes_accessed=8 * length * width * 2,
@@ -391,15 +406,11 @@
     n = len(arrays)
 
     def kernel(*refs):
-        sources, outs, held, sems = refs[:n], refs[n:2 * n], refs[2 * n:3 * n], refs[3 * n]
-        loads = [pltpu.make_async_copy(sources[i], held[i], sems.at[i]) for i in range(n)]
-        stores = [pltpu.make_async_copy(held[i], outs[i], sems.at[n + i]) for i in range(n)]
-        for copy in loads:
+        sources, outs, sems = refs[:n], refs[n:2 * n], refs[2 * n]
+        copies = [pltpu.make_async_copy(sources[i], outs[i], sems.at[i]) for i in range(n)]
+        for copy in copies:
             copy.start()
-        for load, copy in zip(loads, stores):
-            load.wait()
-            copy.start()
-        for copy in stores:
+        for copy in copies:
             copy.wait()
 
     any_ = pl.BlockSpec(memory_space=pl.ANY)
@@ -408,9 +419,8 @@
         out_shape=tuple(jax.ShapeDtypeStruct(x.shape, x.dtype) for x in arrays),
         in_specs=[any_] * n,
         out_specs=(any_,) * n,
-        scratch_shapes=[pltpu.VMEM(x.shape, x.dtype) for x in arrays]
-        + [pltpu.SemaphoreType.DMA((2 * n,))],
-        compiler_params=pltpu.CompilerParams(vmem_limit_bytes=60 * 1024 * 1024),
+        scratch_shapes=[pltpu.SemaphoreType.DMA((n,))],
+        compiler_params=pltpu.CompilerParams(vmem_limit_bytes=4 * 1024 * 1024),
     )(*arrays)
 
 

time: 54.6 us -> 51.7 us (0.947)
  the two profiles are of different devices: /device:TPU:1 before, /device:TPU:12 now
where the time goes in v3:
time: 51.7 us; the launch traced here: 51.4 us
  Pallas kernels  49.4 us (96%)
  local copies, waits for them, and re-layouts  1.39 us (3%)
  between operations  0.65 us (1%)
    pallas_call x1, Pallas kernels, attention(): pl.pallas_call(make_kernel(blocks, peers, length, heads), out_shape=(jax....  48.5 us
    unnamed x4, local copies, waits for them, and re-layouts  1.39 us

profile of v3, /device:TPU:12, one launch (start us, length us, event | category | flops | bytes accessed | tf_op | source)
XLA Modules:
  0.0 51.4 jit_solution(3055248663937875011)
XLA Ops:
  0.6 0.0 copy-start.1
  0.6 0.7 %copy-done.1 = s32[128,3]{0,1:T(4,128)S(1)} copy-done((s32[128,3]{0,1:T(4,128)S(1)}, s32[128,3]{0,1:T(4,128)}, u32[]{:S(2)}) %copy-start.1) | copy-done | bytes 1560
  1.3 0.0 copy-start
  1.3 0.7 %copy-done = f32[4096]{0:T(1024)S(1)} copy-done((f32[4096]{0:T(1024)S(1)}, f32[4096]{0:T(1024)}, u32[]{:S(2)}) %copy-start) | copy-done | bytes 16408
  2.0 48.5 %shard_map.93 = (bf16[16,4096]{1,0:T(8,128)(2,1)S(1)}, bf16[128,512]{1,0:T(8,128)(2,1)S(1)}, bf16[128,512]{1,0:T(8,128)(2,1)S(1)}, bf16[128,512]{1,0:T(8,128)(2,1)S(1)}) custom-call(bf16[128,512]{1,0:T(8,128)(2,1)} %q_hbm.1, bf16[128,512]{1,0:T(8,128)(2,1)} %k_hbm.1, bf16[128,512]{1,0:T(8,128)(2,1)} %v_hbm.1, s32[3,128]{1,0:T(4,128)S(1)} %bitcast.3, ...), custom_call_target="tpu_custom_call" | custom-call | flops 369098752 | bytes 1048576 | tf_op jit(solution)/shard_map/pallas_call | solution.py:373
  50.6 0.8 %shard_map.94 = (bf16[16,4096]{1,0:T(8,128)(2,1)}, bf16[128,512]{1,0:T(8,128)(2,1)}, bf16[128,512]{1,0:T(8,128)(2,1)}, bf16[128,512]{1,0:T(8,128)(2,1)}) custom-call(bf16[16,4096]{1,0:T(8,128)(2,1)S(1)} %get-tuple-element.8.refs_0_, bf16[128,512]{1,0:T(8,128)(2,1)S(1)} %get-tuple-element.9.refs_1_, bf16[128,512]{1,0:T(8,128)(2,1)S(1)} %get-tuple-element.10.refs_2_, ...), custom_call_target="tpu_custom_call" | custom-call | tf_op jit(solution)/shard_map/pallas_call | solution.py:417
Async XLA Ops:
  0.6 0.7 %copy-start.1 = (s32[128,3]{0,1:T(4,128)S(1)}, s32[128,3]{0,1:T(4,128)}, u32[]{:S(2)}) copy-start(s32[128,3]{0,1:T(4,128)} %param.9) | copy-start | bytes 4612
  1.3 0.7 %copy-start = (f32[4096]{0:T(1024)S(1)}, f32[4096]{0:T(1024)}, u32[]{:S(2)}) copy-start(f32[4096]{0:T(1024)} %param.10) | copy-start | bytes 49156

commit v4 on v3

--- a/solution.py
+++ b/solution.py
@@ -245,17 +245,19 @@
 
         my_gain = [gain[:, pl.ds(pl.multiple_of(t * width + h * HSZ, HSZ), HSZ)] for h in range(heads)]
 
+        square = jnp.zeros((length, HSZ), F32)
+        for h in range(heads):
+            value = att[h].astype(F32)
+            square = square + value * value
+        square = jnp.sum(square, -1, keepdims=True)
         with scope("wait_ng"):
             for copy in ng_copies:
                 copy.wait_recv()
-        square = jnp.zeros((length, HSZ), F32)
         cross = jnp.zeros((length, HSZ), F32)
         for h in range(heads):
-            value = att[h].astype(F32)
-            square = square + value * value
-            cross = cross + ng[:, part(h)].astype(F32) * my_gain[h] * value
+            cross = cross + ng[:, part(h)].astype(F32) * my_gain[h] * att[h].astype(F32)
         stats[t] = columns_to_rows(
-            [jnp.sum(square, -1, keepdims=True), jnp.sum(cross, -1, keepdims=True)])
+            [square, jnp.sum(cross, -1, keepdims=True)])
         start(st_copies)
         lse_own[...] = columns_to_rows(lses)
         start(lse_copies)
@@ -368,12 +370,12 @@
     rows = pltpu.VMEM((8, length), F32)
     copies = 3 * heads + 2
     dma = pltpu.SemaphoreType.DMA
-    any_ = pl.BlockSpec(memory_space=pl.ANY)
+    hbm = pl.BlockSpec(memory_space=pltpu.HBM)
     flat = jax.ShapeDtypeStruct((length, width), BF16)
     return pl.pallas_call(
         make_kernel(blocks, peers, length, heads),
         out_shape=(jax.ShapeDtypeStruct((tile, model), BF16), flat, flat, flat),
-        in_specs=[any_, any_, any_, pl.BlockSpec(memory_space=pltpu.SMEM), any_, any_],
+        in_specs=[hbm, hbm, hbm, pl.BlockSpec(memory_space=pltpu.SMEM), hbm, hbm],
         out_specs=(pl.BlockSpec(memory_space=pltpu.VMEM),) * 4,
         scratch_shapes=[head_block] * 13
         + [flat_block]
@@ -399,7 +401,11 @@
             flops=2 * 22 * heads * length * length * HSZ,
             bytes_accessed=8 * length * width * 2,
             transcendentals=5 * heads * length * length),
-    )(queries, key_rows, value_rows, view_mask.T, norm_gain.reshape(1, model), normed_grad)
+    )(*(
+        pltpu.with_memory_space_constraint(x, pltpu.HBM)
+        for x in (
+            queries, key_rows, value_rows, view_mask.T, norm_gain.reshape(1, model), normed_grad)
+    ))
 
 
 def copy_out(*arrays):

time: 51.7 us -> 50.5 us (0.977)
  local copies, waits for them, and re-layouts: 1.39 us -> 0 us
    unnamed x4 -> x0, local copies, waits for them, and re-layouts: 1.39 us -> none
where the time goes in v4:
time: 50.5 us; the launch traced here: 50.2 us
  Pallas kernels  49.6 us (98%)
  between operations  0.64 us (1%)
    pallas_call x1, Pallas kernels, attention(): pl.pallas_call(make_kernel(blocks, peers, length, heads), out_shape=(jax....  48.8 us

profile of v4, /device:TPU:12, one launch (start us, length us, event | category | flops | bytes accessed | tf_op | source)
XLA Modules:
  0.0 50.2 jit_solution(4642675128343944527)
XLA Ops:
  0.6 48.8 %shard_map.93 = (bf16[16,4096]{1,0:T(8,128)(2,1)S(1)}, bf16[128,512]{1,0:T(8,128)(2,1)S(1)}, bf16[128,512]{1,0:T(8,128)(2,1)S(1)}, bf16[128,512]{1,0:T(8,128)(2,1)S(1)}) custom-call(bf16[128,512]{1,0:T(8,128)(2,1)} %q_hbm.1, bf16[128,512]{1,0:T(8,128)(2,1)} %k_hbm.1, bf16[128,512]{1,0:T(8,128)(2,1)} %v_hbm.1, s32[3,128]{1,0:T(4,128)} %bitcast.3, ...), custom_call_target="tpu_custom_call" | custom-call | flops 369098752 | bytes 1048576 | tf_op jit(solution)/shard_map/pallas_call | solution.py:375
  49.4 0.8 %shard_map.94 = (bf16[16,4096]{1,0:T(8,128)(2,1)}, bf16[128,512]{1,0:T(8,128)(2,1)}, bf16[128,512]{1,0:T(8,128)(2,1)}, bf16[128,512]{1,0:T(8,128)(2,1)}) custom-call(bf16[16,4096]{1,0:T(8,128)(2,1)S(1)} %get-tuple-element.8.refs_0_, bf16[128,512]{1,0:T(8,128)(2,1)S(1)} %get-tuple-element.9.refs_1_, bf16[128,512]{1,0:T(8,128)(2,1)S(1)} %get-tuple-element.10.refs_2_, ...), custom_call_target="tpu_custom_call" | custom-call | tf_op jit(solution)/shard_map/pallas_call | solution.py:423

commit v5 on v4

--- a/solution.py
+++ b/solution.py
@@ -307,6 +307,9 @@
                 dq_out[:, part(h)] = (dq * scale).astype(BF16)
                 dk_f[h] = dot_tn(ds[0], q_own[h])
                 dv_f[h] = dot_tn(probs[h, 0].astype(BF16), grad)
+            if h >= 1:
+                for i in ((0,), (1,), (2, 3))[h - 1]:
+                    pass_on(dos[i])
 
         def key_side(h, index, queries, grads, rows):
             grad = grads[h]
@@ -321,8 +324,6 @@
                 relayed[i].wait_recv()
             key_probs(1, q_r, lse_r, from_r)
 
-        for i in dos:
-            pass_on(i)
         with scope("wait_row_p"):
             row_copies[0].wait_recv()
         for h in range(heads):

time: 50.5 us -> 50.5 us (level)
  no operation moved by 1% of the time
where the time goes in v5:
time: 50.5 us; the launch traced here: 50.2 us
  Pallas kernels  49.6 us (98%)
  between operations  0.64 us (1%)
    pallas_call x1, Pallas kernels, attention(): pl.pallas_call(make_kernel(blocks, peers, length, heads), out_shape=(jax....  48.8 us

profile of v5, /device:TPU:12, one launch (start us, length us, event | category | flops | bytes accessed | tf_op | source)
XLA Modules:
  0.0 50.2 jit_solution(11020248592418978654)
XLA Ops:
  0.6 48.8 %shard_map.93 = (bf16[16,4096]{1,0:T(8,128)(2,1)S(1)}, bf16[128,512]{1,0:T(8,128)(2,1)S(1)}, bf16[128,512]{1,0:T(8,128)(2,1)S(1)}, bf16[128,512]{1,0:T(8,128)(2,1)S(1)}) custom-call(bf16[128,512]{1,0:T(8,128)(2,1)} %q_hbm.1, bf16[128,512]{1,0:T(8,128)(2,1)} %k_hbm.1, bf16[128,512]{1,0:T(8,128)(2,1)} %v_hbm.1, s32[3,128]{1,0:T(4,128)} %bitcast.3, ...), custom_call_target="tpu_custom_call" | custom-call | flops 369098752 | bytes 1048576 | tf_op jit(solution)/shard_map/pallas_call | solution.py:376
  49.4 0.8 %shard_map.94 = (bf16[16,4096]{1,0:T(8,128)(2,1)}, bf16[128,512]{1,0:T(8,128)(2,1)}, bf16[128,512]{1,0:T(8,128)(2,1)}, bf16[128,512]{1,0:T(8,128)(2,1)}) custom-call(bf16[16,4096]{1,0:T(8,128)(2,1)S(1)} %get-tuple-element.8.refs_0_, bf16[128,512]{1,0:T(8,128)(2,1)S(1)} %get-tuple-element.9.refs_1_, bf16[128,512]{1,0:T(8,128)(2,1)S(1)} %get-tuple-element.10.refs_2_, ...), custom_call_target="tpu_custom_call" | custom-call | tf_op jit(solution)/shard_map/pallas_call | solution.py:424
